TPU v7x, 32 devices: a whole 2x2x4 slice. The times are simulated.
32 devices in a mesh: seq: 8 (over y, x, core), dp: 4 (over z).
Axes of the slice: x: 2, y: 2, z: 4, core: 2. Of those that a mesh axis runs over, the one named last changes fastest.
Arguments:
- frames: bfloat16 [4, 2048, 1536], P('dp', 'seq'), may hold values from -6 to 6
- lengths: int32 [4], P('dp'), may hold values from 512 to 2048, as said below
- wqkv: bfloat16 [1536, 4608], P(None, 'dp')
- wo: bfloat16 [1536, 1536], replicated, may hold values from -0.15625 to 0.15625
- gain_attn: float32 [1536], replicated, may hold values from 0.1 to 1.9
- gain_conv: float32 [1536], replicated, may hold values from 0.1 to 1.9
- conv_w: float32 [31, 1536], replicated, may hold values from -1 to 1
Outputs:
- block_out: bfloat16 [4, 2048, 1536], P('dp', 'seq')
Inputs may be any that keep to these rules, and one draw needn't show every extreme that they name: `lengths`: at least one utterance has all 2048 frames valid.
All inputs are finite; a program needn't handle non-finite values.
Results may differ from a plain program's by a relative error of at most 0.004.
The roundings to bfloat16 on the way count: a program that leaves them out, or rounds other values in their place, can miss the bound.
Values may be sent and summed in bfloat16 or wider, within the bound.
A program may use at most 64 MiB of HBM per device.

v0:
```python
import jax
import jax.numpy as jnp
from jax import lax
from jax.sharding import PartitionSpec as P

HEADS = 16


def padded_2(array, sides, width):
    for axis, dim in sides:
        count, length = (lax.axis_size(axis), array.shape[dim])
        up = [(i, (i + 1) % count) for i in range(count - 1)]
        down = [(j, i) for i, j in up]
        last = lax.slice_in_dim(array, length - width, length, axis=dim)
        leading = lax.slice_in_dim(array, 0, width, axis=dim)
        before = lax.ppermute(last, axis, up)
        after = lax.ppermute(leading, axis, down)
        array = jnp.concatenate([before, array, after], axis=dim)
    return array


def layer_norm(values, gain):
    values = values.astype(jnp.float32)
    mean = jnp.mean(values, axis=-1, keepdims=True)
    centred = values - mean
    var = jnp.mean(centred * centred, axis=-1, keepdims=True)
    return centred * lax.rsqrt(var + 1e-05) * gain


def attend(query, keys, values, length, head_size):
    scores = jnp.einsum(
        "qhe,khe->hqk", query, keys, preferred_element_type=jnp.float32
    ) * head_size ** (-0.5)
    valid = jnp.arange(keys.shape[0], dtype=jnp.int32) < length
    scores = jnp.where(valid[None, None, :], scores, -1e30)
    top = jnp.max(scores, axis=-1, keepdims=True)
    weights = jnp.exp(scores - top)
    probs = (weights / jnp.sum(weights, axis=-1, keepdims=True)).astype(jnp.bfloat16)
    return jnp.einsum("hqk,khe->qhe", probs, values, preferred_element_type=jnp.float32).astype(
        jnp.bfloat16
    )


def body(frames, lengths, wqkv, wo, gain_attn, gain_conv, conv_w):
    rows = frames[0]
    count = rows.shape[0]
    width = rows.shape[1]
    head_size = width // HEADS
    length = lengths[0]
    normed = layer_norm(rows, gain_attn).astype(jnp.bfloat16)
    qkv = jnp.dot(
        normed, lax.all_gather(wqkv, "dp", axis=1, tiled=True), preferred_element_type=jnp.float32
    ).astype(jnp.bfloat16)
    grouped = qkv.reshape(count, HEADS, 3 * head_size)
    local = lax.all_to_all(grouped, "seq", split_axis=1, concat_axis=0, tiled=True)
    total = local.shape[0]
    local_heads = local.shape[1]
    query = local[:, :, :head_size]
    keys = local[:, :, head_size : 2 * head_size]
    values = local[:, :, 2 * head_size :]
    block = 512
    query_blocks = query.reshape(total // block, block, local_heads, head_size)
    attended = lax.map(
        lambda part_rows: attend(part_rows, keys, values, length, head_size), query_blocks
    )
    attended = attended.reshape(total, local_heads, head_size)
    back = lax.all_to_all(attended, "seq", split_axis=0, concat_axis=1, tiled=True)
    heads_out = back.reshape(count, width)
    mid = rows.astype(jnp.float32) + jnp.dot(heads_out, wo, preferred_element_type=jnp.float32)
    first_frame = lax.axis_index("seq") * count
    positions = first_frame + jnp.arange(count, dtype=jnp.int32)
    valid = (positions < length).astype(jnp.float32)
    conv_in = (layer_norm(mid, gain_conv) * valid[:, None]).astype(jnp.bfloat16)
    reach = (conv_w.shape[0] - 1) // 2
    padded = padded_2(conv_in, (("seq", 0),), reach)
    conv = jnp.zeros((count, width), jnp.float32)
    for tap in range(conv_w.shape[0]):
        conv = conv + conv_w[tap][None, :] * padded[tap : tap + count].astype(jnp.float32)
    result = (mid + conv * jax.nn.sigmoid(conv)).astype(jnp.bfloat16)
    return result[None]


def solution(mesh):
    return jax.shard_map(
        body,
        mesh=mesh,
        in_specs=(P("dp", "seq", None), P("dp"), P(None, "dp"), P(), P(), P(), P()),
        out_specs=P("dp", "seq", None),
        check_vma=False,
    )
```

profile of v0, /device:TPU:3, one launch (start us, length us, event | category | flops | bytes accessed | tf_op | source)
XLA Modules:
  0.0 401.4 jit_solution(8569938863491406058)
XLA Ops:
  6.5 0.0 copy-start
  6.5 0.0 all-gather.2.cloned.1.call-start
  6.5 0.7 all-gather.2.cloned.1.call-update
  7.3 0.4 copy-done
  7.7 0.0 copy-start.4
  7.7 0.2 convert_reduce_fusion
  7.9 0.3 fusion.31
  8.2 246.1 %all-gather.2.cloned.1.call-done = bf16[1536,4608]{1,0:T(8,128)(2,1)} async-done(((bf16[1536,1152]{1,0:T(8,128)(2,1)}), bf16[1536,4608]{1,0:T(8,128)(2,1)}) %all-gather.2.cloned.1.call-update) | async-done | bytes 14155792 | tf_op jit(solution)/shard_map/all_gather | solution.py:52
  254.3 0.0 copy-done.4
  254.3 9.2 %convolution_convert_fusion = bf16[256,4608]{1,0:T(8,128)(2,1)S(1)} fusion(bf16[1536,4608]{1,0:T(8,128)(2,1)} %all-gather.2.cloned.1.call-done, bf16[1,256,1536]{2,1,0:T(8,128)(2,1)S(1)} %copy-done, f32[1536]{0:T(1024)S(1)} %copy-done.4, f32[256]{0:T(256)S(1)} %add_rsqrt_fusion.1, f32[256]{0:T(256)S(1)} %broadcast_multiply_fusion.1), kind=kOutput, calls=%fused_computation.23 | convolution fusion | flops 3627024384 | bytes 17309696 | tf_op jit(solution)/shard_map/dot_general | solution.py:51
  263.6 2.4 copy.23
  266.0 4.3 %all-to-all-start = ((bf16[256,16,288]{0,2,1:T(8,128)(2,1)}), bf16[256,16,288]{0,2,1:T(8,128)(2,1)S(1)}, u32[]{:S(2)}, u32[]{:S(2)}) async-start(bf16[256,16,288]{0,2,1:T(8,128)(2,1)} %bitcast.71), calls=%async_computation | async-start | bytes 4718592 | tf_op jit(solution)/shard_map/all_to_all | solution.py:55
  270.3 27.9 %all-to-all-done = bf16[256,16,288]{0,2,1:T(8,128)(2,1)S(1)} async-done(((bf16[256,16,288]{0,2,1:T(8,128)(2,1)}), bf16[256,16,288]{0,2,1:T(8,128)(2,1)S(1)}, u32[]{:S(2)}, u32[]{:S(2)}) %all-to-all-start) | async-done | bytes 2359328 | tf_op jit(solution)/shard_map/all_to_all | solution.py:55
  298.2 0.3 copy.35
  298.5 0.2 fusion.72
  298.7 0.0 copy-start.1
  298.8 1.0 copy.37
  299.8 0.4 copy-done.1
  300.2 50.0 %while.10 = (s32[]{:T(128)}, bf16[4,512,2,96]{1,3,2,0:T(8,128)(2,1)S(1)}, s32[]{:T(128)}, bf16[4,512,2,96]{1,3,2,0:T(8,128)(2,1)}, bf16[2048,2,96]{0,2,1:T(8,128...) while((s32[]{:T(128)}, bf16[4,512,2,96]{1,3,2,0:T(8,128)(2,1)S(1)}, s32[]{:T(128)}, ...), condition=%wide.region_5.6_spmd, body=%wide.region_2.5_spmd.sunk | while | flops 817991680 | bytes 18756180 | solution.py:63
  300.2 0.7 iota_compare_fusion.2
  300.8 6.9 %fusion.89 = (f32[2,512]{1,0:T(2,128)S(1)}, f32[2,512,2048]{2,1,0:T(8,128)}) fusion(pred[2048]{0:T(1024)(128)(4,1)S(1)} %iota_compare_fusion.2, bf16[2048,2,96]{0,2,1:T(8,128)(2,1)S(1)} %get-tuple-element.173, bf16[4,512,2,96]{1,3,2,0:T(8,128)(2,1)} %get-tuple-element.172, s32[]{:T(128)} %get-tuple-element.162), kind=kOutput, calls=%fused_computation.152.clone.1 | convolution fusion | flops 411043840 | bytes 9378304 | tf_op jit(solution)/shard_map/while/body/eval_jaxpr/sub | solution.py:37
  307.8 4.9 %fusion.90 = bf16[4,512,2,96]{1,3,2,0:T(8,128)(2,1)S(1)} fusion(bf16[4,512,2,96]{1,3,2,0:T(8,128)(2,1)S(1)} %get-tuple-element.163, s32[]{:T(128)} %get-tuple-element.162, bf16[2048,2,96]{0,2,1:T(8,128)(2,1)S(1)} %get-tuple-element.174, f32[2,512,2048]{2,1,0:T(8,128)} %get-tuple-element.153, f32[2,512]{1,0:T(2,128)S(1)} %get-tuple-element.154), kind=kOutput, calls=%fused_computation.11.clone.1 | convolution fusion | flops 406945792 | bytes 9375748 | tf_op jit(solution)/shard_map/while/body/eval_jaxpr/hqk,khe->qhe/dot_general | solution.py:39
  312.7 0.7 iota_compare_fusion.2
  313.3 6.9 %fusion.89 = (f32[2,512]{1,0:T(2,128)S(1)}, f32[2,512,2048]{2,1,0:T(8,128)}) fusion(pred[2048]{0:T(1024)(128)(4,1)S(1)} %iota_compare_fusion.2, bf16[2048,2,96]{0,2,1:T(8,128)(2,1)S(1)} %get-tuple-element.173, bf16[4,512,2,96]{1,3,2,0:T(8,128)(2,1)} %get-tuple-element.172, s32[]{:T(128)} %get-tuple-element.162), kind=kOutput, calls=%fused_computation.152.clone.1 | convolution fusion | flops 411043840 | bytes 9378304 | tf_op jit(solution)/shard_map/while/body/eval_jaxpr/sub | solution.py:37
  320.3 4.9 %fusion.90 = bf16[4,512,2,96]{1,3,2,0:T(8,128)(2,1)S(1)} fusion(bf16[4,512,2,96]{1,3,2,0:T(8,128)(2,1)S(1)} %get-tuple-element.163, s32[]{:T(128)} %get-tuple-element.162, bf16[2048,2,96]{0,2,1:T(8,128)(2,1)S(1)} %get-tuple-element.174, f32[2,512,2048]{2,1,0:T(8,128)} %get-tuple-element.153, f32[2,512]{1,0:T(2,128)S(1)} %get-tuple-element.154), kind=kOutput, calls=%fused_computation.11.clone.1 | convolution fusion | flops 406945792 | bytes 9375748 | tf_op jit(solution)/shard_map/while/body/eval_jaxpr/hqk,khe->qhe/dot_general | solution.py:39
  325.2 0.7 iota_compare_fusion.2
  325.8 6.9 %fusion.89 = (f32[2,512]{1,0:T(2,128)S(1)}, f32[2,512,2048]{2,1,0:T(8,128)}) fusion(pred[2048]{0:T(1024)(128)(4,1)S(1)} %iota_compare_fusion.2, bf16[2048,2,96]{0,2,1:T(8,128)(2,1)S(1)} %get-tuple-element.173, bf16[4,512,2,96]{1,3,2,0:T(8,128)(2,1)} %get-tuple-element.172, s32[]{:T(128)} %get-tuple-element.162), kind=kOutput, calls=%fused_computation.152.clone.1 | convolution fusion | flops 411043840 | bytes 9378304 | tf_op jit(solution)/shard_map/while/body/eval_jaxpr/sub | solution.py:37
  332.8 4.9 %fusion.90 = bf16[4,512,2,96]{1,3,2,0:T(8,128)(2,1)S(1)} fusion(bf16[4,512,2,96]{1,3,2,0:T(8,128)(2,1)S(1)} %get-tuple-element.163, s32[]{:T(128)} %get-tuple-element.162, bf16[2048,2,96]{0,2,1:T(8,128)(2,1)S(1)} %get-tuple-element.174, f32[2,512,2048]{2,1,0:T(8,128)} %get-tuple-element.153, f32[2,512]{1,0:T(2,128)S(1)} %get-tuple-element.154), kind=kOutput, calls=%fused_computation.11.clone.1 | convolution fusion | flops 406945792 | bytes 9375748 | tf_op jit(solution)/shard_map/while/body/eval_jaxpr/hqk,khe->qhe/dot_general | solution.py:39
  337.7 0.7 iota_compare_fusion.2
  338.3 6.9 %fusion.89 = (f32[2,512]{1,0:T(2,128)S(1)}, f32[2,512,2048]{2,1,0:T(8,128)}) fusion(pred[2048]{0:T(1024)(128)(4,1)S(1)} %iota_compare_fusion.2, bf16[2048,2,96]{0,2,1:T(8,128)(2,1)S(1)} %get-tuple-element.173, bf16[4,512,2,96]{1,3,2,0:T(8,128)(2,1)} %get-tuple-element.172, s32[]{:T(128)} %get-tuple-element.162), kind=kOutput, calls=%fused_computation.152.clone.1 | convolution fusion | flops 411043840 | bytes 9378304 | tf_op jit(solution)/shard_map/while/body/eval_jaxpr/sub | solution.py:37
  345.3 4.9 %fusion.90 = bf16[4,512,2,96]{1,3,2,0:T(8,128)(2,1)S(1)} fusion(bf16[4,512,2,96]{1,3,2,0:T(8,128)(2,1)S(1)} %get-tuple-element.163, s32[]{:T(128)} %get-tuple-element.162, bf16[2048,2,96]{0,2,1:T(8,128)(2,1)S(1)} %get-tuple-element.174, f32[2,512,2048]{2,1,0:T(8,128)} %get-tuple-element.153, f32[2,512]{1,0:T(2,128)S(1)} %get-tuple-element.154), kind=kOutput, calls=%fused_computation.11.clone.1 | convolution fusion | flops 406945792 | bytes 9375748 | tf_op jit(solution)/shard_map/while/body/eval_jaxpr/hqk,khe->qhe/dot_general | solution.py:39
  350.2 0.0 copy-start.2
  350.2 2.0 copy.30
  352.2 5.1 %all-to-all-start.1 = ((bf16[2048,2,96]{2,1,0:T(2,128)(2,1)}), bf16[2048,2,96]{2,1,0:T(2,128)(2,1)S(1)}, u32[]{:S(2)}, u32[]{:S(2)}) async-start(bf16[2048,2,96]{2,1,0:T(2,128)(2,1)} %bitcast.8), calls=%async_computation.1 | async-start | bytes 2097152 | tf_op jit(solution)/shard_map/all_to_all | solution.py:67
  357.9 0.0 copy-done.2
  357.9 0.3 slice_reduce_fusion.30
  358.2 12.8 %all-to-all-done.1 = bf16[2048,2,96]{2,1,0:T(2,128)(2,1)S(1)} async-done(((bf16[2048,2,96]{2,1,0:T(2,128)(2,1)}), bf16[2048,2,96]{2,1,0:T(2,128)(2,1)S(1)}, u32[]{:S(2)}, u32[]{:S(2)}) %all-to-all-start.1) | async-done | bytes 786464 | tf_op jit(solution)/shard_map/all_to_all | solution.py:67
  371.1 0.7 copy.32
  371.7 3.8 fusion.74
  375.6 0.0 copy-start.3
  375.6 0.3 multiply_reduce_fusion
  375.9 0.4 copy-done.3
  376.3 0.4 multiply_convert_fusion
  376.7 3.5 collective-permute-start
  380.1 1.9 collective-permute-start.1
  382.1 0.2 slice_reduce_fusion.29
  382.3 0.0 collective-permute-done
  382.3 4.2 %collective-permute-done.1 = bf16[15,1536]{1,0:T(8,128)(2,1)S(1)} collective-permute-done((bf16[15,1536]{1,0:T(8,128)(2,1)S(1)}, bf16[15,1536]{1,0:T(8,128)(2,1)S(1)}, u32[]{:S(2)}, u32[]{:S(2)}) %collective-permute-start.1) | collective-permute-done | bytes 46112 | tf_op jit(solution)/shard_map/ppermute | solution.py:17
  386.4 8.2 %fusion.66 = bf16[1,256,1536]{2,1,0:T(8,128)(2,1)} fusion(f32[256,1536]{1,0:T(8,128)S(1)} %get-tuple-element.113, bf16[15,1536]{1,0:T(8,128)(2,1)S(1)} %collective-permute-done.1, bf16[256,1536]{1,0:T(8,128)(2,1)S(1)} %multiply_convert_fusion, f32[1536]{0:T(1024)S(1)} %get-tuple-element.91, f32[1536]{0:T(1024)S(1)} %get-tuple-element.92, ...), kind=kLoop, calls=%fused_computation.115 | loop fusion | flops 73924608 | bytes 3428352 | tf_op jit(solution)/shard_map/broadcast_in_dim | solution.py:80
  (7 shorter events, 0.0 us)
Async XLA Ops:
  6.5 1.1 copy-start
  6.5 247.8 %all-gather.2.cloned.1.call-start = ((), (), s32[]{:S(2)}) async-start(), calls=%async_computation.2 | async-start | bytes 17694720 | tf_op jit(solution)/shard_map/all_gather | solution.py:52
  7.7 246.7 %copy-start.4 = (f32[1536]{0:T(1024)S(1)}, f32[1536]{0:T(1024)}, u32[]{:S(2)}) copy-start(f32[1536]{0:T(1024)} %param.13) | copy-start | bytes 18436
  266.0 32.2 %all-to-all-start = ((bf16[256,16,288]{0,2,1:T(8,128)(2,1)}), bf16[256,16,288]{0,2,1:T(8,128)(2,1)S(1)}, u32[]{:S(2)}, u32[]{:S(2)}) async-start(bf16[256,16,288]{0,2,1:T(8,128)(2,1)} %bitcast.71), calls=%async_computation | async-start | bytes 4718592 | tf_op jit(solution)/shard_map/all_to_all | solution.py:55
  298.7 1.4 copy-start.1
  350.2 7.7 %copy-start.2 = (f32[31,1536]{1,0:T(8,128)S(1)}, f32[31,1536]{1,0:T(8,128)}, u32[]{:S(2)}) copy-start(f32[31,1536]{1,0:T(8,128)} %param.15) | copy-start | bytes 571396
  352.2 18.9 %all-to-all-start.1 = ((bf16[2048,2,96]{2,1,0:T(2,128)(2,1)}), bf16[2048,2,96]{2,1,0:T(2,128)(2,1)S(1)}, u32[]{:S(2)}, u32[]{:S(2)}) async-start(bf16[2048,2,96]{2,1,0:T(2,128)(2,1)} %bitcast.8), calls=%async_computation.1 | async-start | bytes 2097152 | tf_op jit(solution)/shard_map/all_to_all | solution.py:67
  375.6 0.7 copy-start.3
  376.7 5.6 %collective-permute-start = (bf16[15,1536]{1,0:T(8,128)(2,1)S(1)}, bf16[15,1536]{1,0:T(8,128)(2,1)S(1)}, u32[]{:S(2)}, u32[]{:S(2)}) collective-permute-start(bf16[15,1536]{1,0:T(8,128)(2,1)S(1)} %get-tuple-element.110), channel_id=1, source_target_pairs={{0,4},{4,8},{8,12},{12,16},{16,20},{20,24},{24,28},{1,5},{5,9},{9,... | collective-permute-start | bytes 138248 | tf_op jit(solution)/shard_map/ppermute | solution.py:16
  380.1 6.3 %collective-permute-start.1 = (bf16[15,1536]{1,0:T(8,128)(2,1)S(1)}, bf16[15,1536]{1,0:T(8,128)(2,1)S(1)}, u32[]{:S(2)}, u32[]{:S(2)}) collective-permute-start(bf16[15,1536]{1,0:T(8,128)(2,1)S(1)} %get-tuple-element.111), channel_id=1, source_target_pairs={{4,0},{8,4},{12,8},{16,12},{20,16},{24,20},{28,24},{5,1},{9,5},{13... | collective-permute-start | bytes 138248 | tf_op jit(solution)/shard_map/ppermute | solution.py:17
Sparse Core Ops, SparseCore 0:
  8.9 245.3 all-gather.1
where the time goes:
time: 402 us; the launch traced here: 401 us
  waiting for transfers between devices  292 us (73%)
  matrix products  60.3 us (15%)
  starting transfers between devices  14.7 us (4%)
  between operations  14.2 us (4%)
  other arithmetic  12 us (3%)
  local copies, waits for them, and re-layouts  8.37 us (2%)
    all_gather x1, waiting for transfers between devices, body(): lax.all_gather(wqkv, 'dp', axis=1, tiled=True)  246 us
    all_to_all x1, waiting for transfers between devices, body(): lax.all_to_all(grouped, 'seq', split_axis=1, concat_axis=0, tiled=True)  27.9 us
    sub x4, matrix products, attend(): weights = jnp.exp(scores - top)  27.7 us
    dot_general x4, matrix products, attend(): jnp.einsum('hqk,khe->qhe', probs, values, preferred_element_type=jnp.floa...  19.6 us
    all_to_all x1, waiting for transfers between devices, body(): lax.all_to_all(attended, 'seq', split_axis=0, concat_axis=1, tiled=True)  12.8 us
    dot_general x1, matrix products, body(): jnp.dot(normed, lax.all_gather(wqkv, 'dp', axis=1, tiled=True), preferred...  9.23 us
    broadcast_in_dim x1, other arithmetic, body(): return result[None]  8.17 us
  transfers between devices with their start and end apart: 5, of which 4 were waited for; matrix products, arithmetic and copies ran while one was open for 0% of the time, Pallas kernels for 0%

commit v1 on v0

--- a/solution.py
+++ b/solution.py
@@ -64,7 +64,19 @@
         lambda part_rows: attend(part_rows, keys, values, length, head_size), query_blocks
     )
     attended = attended.reshape(total, local_heads, head_size)
-    back = lax.all_to_all(attended, "seq", split_axis=0, concat_axis=1, tiled=True)
+    ways, here = (lax.axis_size("seq"), lax.axis_index("seq"))
+    width_2 = attended.shape[0] // ways
+    lengths_2 = list(attended.shape)
+    lengths_2[0] = width_2
+    height = lengths_2[1]
+    lengths_2[1] = height * ways
+    full = jnp.zeros(lengths_2, attended.dtype)
+    for mask in range(ways):
+        part = lax.dynamic_slice_in_dim(attended, (here ^ mask) * width_2, width_2, axis=0)
+        if mask:
+            part = lax.ppermute(part, "seq", [(d, d ^ mask) for d in range(ways)])
+        full = lax.dynamic_update_slice_in_dim(full, part, (here ^ mask) * height, axis=1)
+    back = full
     heads_out = back.reshape(count, width)
     mid = rows.astype(jnp.float32) + jnp.dot(heads_out, wo, preferred_element_type=jnp.float32)
     first_frame = lax.axis_index("seq") * count

time: 402 us -> 394 us (0.980)
  waiting for transfers between devices: 292 us -> 284 us
    all_to_all x1 -> x0, waiting for transfers between devices: 12.8 us -> none  [body(): lax.all_to_all(attended, 'seq', split_axis=0, concat_axis=1, tiled=True)]
    ppermute x0 -> x7, starting transfers between devices: none -> 7.28 us  [body(): part = lax.ppermute(part, 'seq', [(d, d ^ mask) for d in range(ways)])]
    ppermute x0 -> x7, waiting for transfers between devices: none -> 5.72 us  [body(): part = lax.ppermute(part, 'seq', [(d, d ^ mask) for d in range(ways)])]
    all_to_all x1 -> x0, starting transfers between devices: 5.06 us -> none  [body(): lax.all_to_all(attended, 'seq', split_axis=0, concat_axis=1, tiled=True)]
  transfers between devices with their start and end apart: 5 -> 11, of which waited for: 4 -> 5; matrix products, arithmetic and copies ran while one was open for 0% -> 0% of each run, Pallas kernels for 0% -> 0%
where the time goes in v1:
time: 394 us; the launch traced here: 393 us
  waiting for transfers between devices  284 us (72%)
  matrix products  60.6 us (15%)
  starting transfers between devices  16.8 us (4%)
  between operations  14.3 us (4%)
  other arithmetic  12 us (3%)
  local copies, waits for them, and re-layouts  6.06 us (2%)
    all_gather x1, waiting for transfers between devices, body(): lax.all_gather(wqkv, 'dp', axis=1, tiled=True)  246 us
    sub x4, matrix products, attend(): weights = jnp.exp(scores - top)  27.8 us
    all_to_all x1, waiting for transfers between devices, body(): lax.all_to_all(grouped, 'seq', split_axis=1, concat_axis=0, tiled=True)  26.8 us
    dot_general x4, matrix products, attend(): jnp.einsum('hqk,khe->qhe', probs, values, preferred_element_type=jnp.floa...  19.7 us
    dot_general x1, matrix products, body(): jnp.dot(normed, lax.all_gather(wqkv, 'dp', axis=1, tiled=True), preferred...  9.24 us
    broadcast_in_dim x1, other arithmetic, body(): return result[None]  8.17 us
  transfers between devices with their start and end apart: 11, of which 5 were waited for; matrix products, arithmetic and copies ran while one was open for 0% of the time, Pallas kernels for 0%

profile of v1, /device:TPU:3, one launch (start us, length us, event | category | flops | bytes accessed | tf_op | source)
XLA Modules:
  0.0 393.4 jit_solution(12702874478678972580)
XLA Ops:
  6.5 0.0 copy-start
  6.5 0.0 all-gather.2.cloned.1.call-start
  6.5 0.7 all-gather.2.cloned.1.call-update
  7.3 0.4 copy-done
  7.7 0.0 copy-start.4
  7.7 0.2 convert_reduce_fusion
  7.9 0.3 fusion.31
  8.2 246.1 %all-gather.2.cloned.1.call-done = bf16[1536,4608]{1,0:T(8,128)(2,1)} async-done(((bf16[1536,1152]{1,0:T(8,128)(2,1)}), bf16[1536,4608]{1,0:T(8,128)(2,1)}) %all-gather.2.cloned.1.call-update) | async-done | bytes 14155792 | tf_op jit(solution)/shard_map/all_gather | solution.py:52
  254.3 0.0 copy-done.4
  254.3 9.2 %convolution_convert_fusion = bf16[256,4608]{1,0:T(8,128)(2,1)S(1)} fusion(bf16[1536,4608]{1,0:T(8,128)(2,1)} %all-gather.2.cloned.1.call-done, bf16[1,256,1536]{2,1,0:T(8,128)(2,1)S(1)} %copy-done, f32[1536]{0:T(1024)S(1)} %copy-done.4, f32[256]{0:T(256)S(1)} %add_rsqrt_fusion.1, f32[256]{0:T(256)S(1)} %broadcast_multiply_fusion.1), kind=kOutput, calls=%fused_computation.23 | convolution fusion | flops 3627024384 | bytes 17309696 | tf_op jit(solution)/shard_map/dot_general | solution.py:51
  263.6 2.4 copy.12
  266.0 0.0 copy-start.2
  266.0 4.4 %all-to-all-start = ((bf16[256,16,288]{0,2,1:T(8,128)(2,1)}), bf16[256,16,288]{0,2,1:T(8,128)(2,1)S(1)}, u32[]{:S(2)}, u32[]{:S(2)}) async-start(bf16[256,16,288]{0,2,1:T(8,128)(2,1)} %bitcast.68), calls=%async_computation | async-start | bytes 4718592 | tf_op jit(solution)/shard_map/all_to_all | solution.py:55
  271.2 0.0 copy-done.2
  271.2 0.3 slice_reduce_fusion.30
  271.5 26.8 %all-to-all-done = bf16[256,16,288]{0,2,1:T(8,128)(2,1)S(1)} async-done(((bf16[256,16,288]{0,2,1:T(8,128)(2,1)}), bf16[256,16,288]{0,2,1:T(8,128)(2,1)S(1)}, u32[]{:S(2)}, u32[]{:S(2)}) %all-to-all-start) | async-done | bytes 2359328 | tf_op jit(solution)/shard_map/all_to_all | solution.py:55
  298.3 0.3 copy.17
  298.6 0.2 fusion.72
  298.9 0.0 copy-start.1
  298.9 1.0 copy.20
  299.9 0.4 copy-done.1
  300.3 50.2 %while.10 = (s32[]{:T(128)}, bf16[4,512,2,96]{1,3,2,0:T(8,128)(2,1)S(1)}, s32[]{:T(128)}, bf16[4,512,2,96]{1,3,2,0:T(8,128)(2,1)}, bf16[2048,2,96]{0,2,1:T(8,128...) while((s32[]{:T(128)}, bf16[4,512,2,96]{1,3,2,0:T(8,128)(2,1)S(1)}, s32[]{:T(128)}, ...), condition=%wide.region_5.6_spmd, body=%wide.region_2.5_spmd.sunk | while | flops 817991680 | bytes 18756180 | solution.py:63
  300.3 0.7 iota_compare_fusion.2
  300.9 7.0 %fusion.89 = (f32[2,512]{1,0:T(2,128)S(1)}, f32[2,512,2048]{2,1,0:T(8,128)}) fusion(pred[2048]{0:T(1024)(128)(4,1)S(1)} %iota_compare_fusion.2, bf16[2048,2,96]{0,2,1:T(8,128)(2,1)S(1)} %get-tuple-element.169, bf16[4,512,2,96]{1,3,2,0:T(8,128)(2,1)} %get-tuple-element.168, s32[]{:T(128)} %get-tuple-element.158), kind=kOutput, calls=%fused_computation.167.clone.1 | convolution fusion | flops 411043840 | bytes 9378304 | tf_op jit(solution)/shard_map/while/body/eval_jaxpr/sub | solution.py:37
  307.9 4.9 %fusion.90 = bf16[4,512,2,96]{1,3,2,0:T(8,128)(2,1)S(1)} fusion(bf16[4,512,2,96]{1,3,2,0:T(8,128)(2,1)S(1)} %get-tuple-element.159, s32[]{:T(128)} %get-tuple-element.158, bf16[2048,2,96]{0,2,1:T(8,128)(2,1)S(1)} %get-tuple-element.170, f32[2,512,2048]{2,1,0:T(8,128)} %get-tuple-element.149, f32[2,512]{1,0:T(2,128)S(1)} %get-tuple-element.150), kind=kOutput, calls=%fused_computation.11.clone.1 | convolution fusion | flops 406945792 | bytes 9375748 | tf_op jit(solution)/shard_map/while/body/eval_jaxpr/hqk,khe->qhe/dot_general | solution.py:39
  312.8 0.7 iota_compare_fusion.2
  313.5 7.0 %fusion.89 = (f32[2,512]{1,0:T(2,128)S(1)}, f32[2,512,2048]{2,1,0:T(8,128)}) fusion(pred[2048]{0:T(1024)(128)(4,1)S(1)} %iota_compare_fusion.2, bf16[2048,2,96]{0,2,1:T(8,128)(2,1)S(1)} %get-tuple-element.169, bf16[4,512,2,96]{1,3,2,0:T(8,128)(2,1)} %get-tuple-element.168, s32[]{:T(128)} %get-tuple-element.158), kind=kOutput, calls=%fused_computation.167.clone.1 | convolution fusion | flops 411043840 | bytes 9378304 | tf_op jit(solution)/shard_map/while/body/eval_jaxpr/sub | solution.py:37
  320.5 4.9 %fusion.90 = bf16[4,512,2,96]{1,3,2,0:T(8,128)(2,1)S(1)} fusion(bf16[4,512,2,96]{1,3,2,0:T(8,128)(2,1)S(1)} %get-tuple-element.159, s32[]{:T(128)} %get-tuple-element.158, bf16[2048,2,96]{0,2,1:T(8,128)(2,1)S(1)} %get-tuple-element.170, f32[2,512,2048]{2,1,0:T(8,128)} %get-tuple-element.149, f32[2,512]{1,0:T(2,128)S(1)} %get-tuple-element.150), kind=kOutput, calls=%fused_computation.11.clone.1 | convolution fusion | flops 406945792 | bytes 9375748 | tf_op jit(solution)/shard_map/while/body/eval_jaxpr/hqk,khe->qhe/dot_general | solution.py:39
  325.4 0.7 iota_compare_fusion.2
  326.0 7.0 %fusion.89 = (f32[2,512]{1,0:T(2,128)S(1)}, f32[2,512,2048]{2,1,0:T(8,128)}) fusion(pred[2048]{0:T(1024)(128)(4,1)S(1)} %iota_compare_fusion.2, bf16[2048,2,96]{0,2,1:T(8,128)(2,1)S(1)} %get-tuple-element.169, bf16[4,512,2,96]{1,3,2,0:T(8,128)(2,1)} %get-tuple-element.168, s32[]{:T(128)} %get-tuple-element.158), kind=kOutput, calls=%fused_computation.167.clone.1 | convolution fusion | flops 411043840 | bytes 9378304 | tf_op jit(solution)/shard_map/while/body/eval_jaxpr/sub | solution.py:37
  333.0 4.9 %fusion.90 = bf16[4,512,2,96]{1,3,2,0:T(8,128)(2,1)S(1)} fusion(bf16[4,512,2,96]{1,3,2,0:T(8,128)(2,1)S(1)} %get-tuple-element.159, s32[]{:T(128)} %get-tuple-element.158, bf16[2048,2,96]{0,2,1:T(8,128)(2,1)S(1)} %get-tuple-element.170, f32[2,512,2048]{2,1,0:T(8,128)} %get-tuple-element.149, f32[2,512]{1,0:T(2,128)S(1)} %get-tuple-element.150), kind=kOutput, calls=%fused_computation.11.clone.1 | convolution fusion | flops 406945792 | bytes 9375748 | tf_op jit(solution)/shard_map/while/body/eval_jaxpr/hqk,khe->qhe/dot_general | solution.py:39
  337.9 0.7 iota_compare_fusion.2
  338.6 7.0 %fusion.89 = (f32[2,512]{1,0:T(2,128)S(1)}, f32[2,512,2048]{2,1,0:T(8,128)}) fusion(pred[2048]{0:T(1024)(128)(4,1)S(1)} %iota_compare_fusion.2, bf16[2048,2,96]{0,2,1:T(8,128)(2,1)S(1)} %get-tuple-element.169, bf16[4,512,2,96]{1,3,2,0:T(8,128)(2,1)} %get-tuple-element.168, s32[]{:T(128)} %get-tuple-element.158), kind=kOutput, calls=%fused_computation.167.clone.1 | convolution fusion | flops 411043840 | bytes 9378304 | tf_op jit(solution)/shard_map/while/body/eval_jaxpr/sub | solution.py:37
  345.6 4.9 %fusion.90 = bf16[4,512,2,96]{1,3,2,0:T(8,128)(2,1)S(1)} fusion(bf16[4,512,2,96]{1,3,2,0:T(8,128)(2,1)S(1)} %get-tuple-element.159, s32[]{:T(128)} %get-tuple-element.158, bf16[2048,2,96]{0,2,1:T(8,128)(2,1)S(1)} %get-tuple-element.170, f32[2,512,2048]{2,1,0:T(8,128)} %get-tuple-element.149, f32[2,512]{1,0:T(2,128)S(1)} %get-tuple-element.150), kind=kOutput, calls=%fused_computation.11.clone.1 | convolution fusion | flops 406945792 | bytes 9375748 | tf_op jit(solution)/shard_map/while/body/eval_jaxpr/hqk,khe->qhe/dot_general | solution.py:39
  350.5 0.1 copy.18
  350.6 0.1 broadcast_in_dim.25
  350.7 0.1 constant_dynamic-slice_fusion
  350.8 0.5 collective-permute-start
  351.3 1.2 collective-permute-start.1
  352.6 0.5 collective-permute-start.2
  353.0 0.4 collective-permute-start.3
  353.4 1.4 collective-permute-start.4
  354.8 0.0 collective-permute-done
  354.8 1.2 collective-permute-start.5
  356.1 0.0 collective-permute-done.1
  356.1 2.0 collective-permute-start.6
  358.1 0.6 collective-permute-done.2
  358.7 0.0 collective-permute-done.3
  358.8 5.1 %collective-permute-done.4 = bf16[256,2,96]{0,2,1:T(8,128)(2,1)S(1)} collective-permute-done((bf16[256,2,96]{0,2,1:T(8,128)(2,1)S(1)}, bf16[256,2,96]{0,2,1:T(8,128)(2,1)S(1)}, u32[]{:S(2)}, u32[]{:S(2)}) %collective-permute-start.4) | collective-permute-done | bytes 98336 | tf_op jit(solution)/shard_map/ppermute | solution.py:77
  363.9 0.0 collective-permute-done.5
  363.9 0.0 collective-permute-done.6
  364.0 3.8 fusion.74
  367.8 0.0 copy-start.3
  367.8 0.3 multiply_reduce_fusion
  368.1 0.4 copy-done.3
  368.5 0.4 multiply_convert_fusion
  368.9 3.1 collective-permute-start.7
  372.0 1.9 collective-permute-start.8
  374.0 0.2 slice_reduce_fusion.29
  374.2 0.0 collective-permute-done.7
  374.2 4.2 %collective-permute-done.8 = bf16[15,1536]{1,0:T(8,128)(2,1)S(1)} collective-permute-done((bf16[15,1536]{1,0:T(8,128)(2,1)S(1)}, bf16[15,1536]{1,0:T(8,128)(2,1)S(1)}, u32[]{:S(2)}, u32[]{:S(2)}) %collective-permute-start.8) | collective-permute-done | bytes 46112 | tf_op jit(solution)/shard_map/ppermute | solution.py:17
  378.3 8.2 %fusion.66 = bf16[1,256,1536]{2,1,0:T(8,128)(2,1)} fusion(f32[256,1536]{1,0:T(8,128)S(1)} %get-tuple-element.109, bf16[15,1536]{1,0:T(8,128)(2,1)S(1)} %collective-permute-done.8, bf16[256,1536]{1,0:T(8,128)(2,1)S(1)} %multiply_convert_fusion, f32[1536]{0:T(1024)S(1)} %get-tuple-element.79, f32[1536]{0:T(1024)S(1)} %get-tuple-element.80, ...), kind=kLoop, calls=%fused_computation.115 | loop fusion | flops 73924608 | bytes 3428352 | tf_op jit(solution)/shard_map/broadcast_in_dim | solution.py:92
  (14 shorter events, 0.1 us)
Async XLA Ops:
  6.5 1.1 copy-start
  6.5 247.8 %all-gather.2.cloned.1.call-start = ((), (), s32[]{:S(2)}) async-start(), calls=%async_computation.1 | async-start | bytes 17694720 | tf_op jit(solution)/shard_map/all_gather | solution.py:52
  7.7 246.7 %copy-start.4 = (f32[1536]{0:T(1024)S(1)}, f32[1536]{0:T(1024)}, u32[]{:S(2)}) copy-start(f32[1536]{0:T(1024)} %param.13) | copy-start | bytes 18436
  266.0 5.2 %copy-start.2 = (f32[31,1536]{1,0:T(8,128)S(1)}, f32[31,1536]{1,0:T(8,128)}, u32[]{:S(2)}) copy-start(f32[31,1536]{1,0:T(8,128)} %param.15) | copy-start | bytes 571396
  266.0 32.3 %all-to-all-start = ((bf16[256,16,288]{0,2,1:T(8,128)(2,1)}), bf16[256,16,288]{0,2,1:T(8,128)(2,1)S(1)}, u32[]{:S(2)}, u32[]{:S(2)}) async-start(bf16[256,16,288]{0,2,1:T(8,128)(2,1)} %bitcast.68), calls=%async_computation | async-start | bytes 4718592 | tf_op jit(solution)/shard_map/all_to_all | solution.py:55
  298.9 1.4 copy-start.1
  350.8 4.0 %collective-permute-start = (bf16[256,2,96]{0,2,1:T(8,128)(2,1)S(1)}, bf16[256,2,96]{0,2,1:T(8,128)(2,1)S(1)}, u32[]{:S(2)}, u32[]{:S(2)}) collective-permute-start(bf16[256,2,96]{0,2,1:T(8,128)(2,1)S(1)} %get-tuple-element.106), channel_id=1, source_target_pairs={{0,4},{4,0},{8,12},{12,8},{16,20},{20,16},{24,28},{28,24},{1,5},{5... | collective-permute-start | bytes 294920 | tf_op jit(solution)/shard_map/ppermute | solution.py:77
  351.3 4.7 %collective-permute-start.1 = (bf16[256,2,96]{0,2,1:T(8,128)(2,1)S(1)}, bf16[256,2,96]{0,2,1:T(8,128)(2,1)S(1)}, u32[]{:S(2)}, u32[]{:S(2)}) collective-permute-start(bf16[256,2,96]{0,2,1:T(8,128)(2,1)S(1)} %get-tuple-element.105), channel_id=1, source_target_pairs={{0,8},{4,12},{8,0},{12,4},{16,24},{20,28},{24,16},{28,20},{1,9},{5... | collective-permute-start | bytes 294920 | tf_op jit(solution)/shard_map/ppermute | solution.py:77
  352.6 6.2 %collective-permute-start.2 = (bf16[256,2,96]{0,2,1:T(8,128)(2,1)S(1)}, bf16[256,2,96]{0,2,1:T(8,128)(2,1)S(1)}, u32[]{:S(2)}, u32[]{:S(2)}) collective-permute-start(bf16[256,2,96]{0,2,1:T(8,128)(2,1)S(1)} %get-tuple-element.104), channel_id=1, source_target_pairs={{0,12},{4,8},{8,4},{12,0},{16,28},{20,24},{24,20},{28,16},{1,13},{... | collective-permute-start | bytes 294920 | tf_op jit(solution)/shard_map/ppermute | solution.py:77
  353.0 5.7 %collective-permute-start.3 = (bf16[256,2,96]{0,2,1:T(8,128)(2,1)S(1)}, bf16[256,2,96]{0,2,1:T(8,128)(2,1)S(1)}, u32[]{:S(2)}, u32[]{:S(2)}) collective-permute-start(bf16[256,2,96]{0,2,1:T(8,128)(2,1)S(1)} %get-tuple-element.103), channel_id=1, source_target_pairs={{0,16},{4,20},{8,24},{12,28},{16,0},{20,4},{24,8},{28,12},{1,17},{... | collective-permute-start | bytes 294920 | tf_op jit(solution)/shard_map/ppermute | solution.py:77
  353.4 10.5 %collective-permute-start.4 = (bf16[256,2,96]{0,2,1:T(8,128)(2,1)S(1)}, bf16[256,2,96]{0,2,1:T(8,128)(2,1)S(1)}, u32[]{:S(2)}, u32[]{:S(2)}) collective-permute-start(bf16[256,2,96]{0,2,1:T(8,128)(2,1)S(1)} %get-tuple-element.102), channel_id=1, source_target_pairs={{0,20},{4,16},{8,28},{12,24},{16,4},{20,0},{24,12},{28,8},{1,21},{... | collective-permute-start | bytes 294920 | tf_op jit(solution)/shard_map/ppermute | solution.py:77
  354.8 9.1 %collective-permute-start.5 = (bf16[256,2,96]{0,2,1:T(8,128)(2,1)S(1)}, bf16[256,2,96]{0,2,1:T(8,128)(2,1)S(1)}, u32[]{:S(2)}, u32[]{:S(2)}) collective-permute-start(bf16[256,2,96]{0,2,1:T(8,128)(2,1)S(1)} %get-tuple-element.101), channel_id=1, source_target_pairs={{0,24},{4,28},{8,16},{12,20},{16,8},{20,12},{24,0},{28,4},{1,25},{... | collective-permute-start | bytes 294920 | tf_op jit(solution)/shard_map/ppermute | solution.py:77
  356.1 7.9 %collective-permute-start.6 = (bf16[256,2,96]{0,2,1:T(8,128)(2,1)S(1)}, bf16[256,2,96]{0,2,1:T(8,128)(2,1)S(1)}, u32[]{:S(2)}, u32[]{:S(2)}) collective-permute-start(bf16[256,2,96]{0,2,1:T(8,128)(2,1)S(1)} %get-tuple-element.100), channel_id=1, source_target_pairs={{0,28},{4,24},{8,20},{12,16},{16,12},{20,8},{24,4},{28,0},{1,29},{... | collective-permute-start | bytes 294920 | tf_op jit(solution)/shard_map/ppermute | solution.py:77
  367.8 0.7 copy-start.3
  368.9 5.3 %collective-permute-start.7 = (bf16[15,1536]{1,0:T(8,128)(2,1)S(1)}, bf16[15,1536]{1,0:T(8,128)(2,1)S(1)}, u32[]{:S(2)}, u32[]{:S(2)}) collective-permute-start(bf16[15,1536]{1,0:T(8,128)(2,1)S(1)} %get-tuple-element.98), channel_id=1, source_target_pairs={{0,4},{4,8},{8,12},{12,16},{16,20},{20,24},{24,28},{1,5},{5,9},{9,... | collective-permute-start | bytes 138248 | tf_op jit(solution)/shard_map/ppermute | solution.py:16
  372.0 6.3 %collective-permute-start.8 = (bf16[15,1536]{1,0:T(8,128)(2,1)S(1)}, bf16[15,1536]{1,0:T(8,128)(2,1)S(1)}, u32[]{:S(2)}, u32[]{:S(2)}) collective-permute-start(bf16[15,1536]{1,0:T(8,128)(2,1)S(1)} %get-tuple-element.99), channel_id=1, source_target_pairs={{4,0},{8,4},{12,8},{16,12},{20,16},{24,20},{28,24},{5,1},{9,5},{13... | collective-permute-start | bytes 138248 | tf_op jit(solution)/shard_map/ppermute | solution.py:17
Sparse Core Ops, SparseCore 0:
  8.9 245.3 all-gather.1
